TPU v7x, 512 devices: a whole 4x8x8 slice. The times are simulated.
512 devices in a mesh: ctx: 128 (over z, y_lo, x), head: 4 (over y_hi, core).
Axes of the slice: x: 4, y: 8 (y_hi: 2, y_lo: 4; y = y_hi * 4 + y_lo), z: 8, core: 2. Of those that a mesh axis runs over, the one named last changes fastest.
Arguments:
- queries: bfloat16 [65536, 1024], P('ctx', 'head'), may hold values from -6 to 6
- key_rows: bfloat16 [65536, 1024], P('ctx', 'head'), may hold values from -6 to 6
- value_rows: bfloat16 [65536, 1024], P('ctx', 'head'), may hold values from -6 to 6
- gating: bfloat16 [65536, 1024], P('ctx', 'head'), may hold values from -6 to 6
- gain_vector: bfloat16 [1024], P('head'), may hold values from 0.099609375 to 1.8984375
- out_grad: bfloat16 [65536, 1024], P('ctx', 'head'), may hold values from -6 to 6
- user_lengths: int32 [4], replicated, may hold values from 1 to 32768, 65536 in all
- cand_counts: int32 [4], replicated, may hold values from 1 to 256
Outputs:
- output: bfloat16 [65536, 1024], P('ctx', 'head')
- query_grad: bfloat16 [65536, 1024], P('ctx', 'head')
- key_grad: bfloat16 [65536, 1024], P('ctx', 'head')
- value_grad: bfloat16 [65536, 1024], P('ctx', 'head')
- gate_grad: bfloat16 [65536, 1024], P('ctx', 'head')
Inputs may be any that keep to these rules, and one draw needn't show every extreme that they name: user_lengths sum to 65536; the longest user has exactly 32768 tokens. `cand_counts`: a user's last min(count, length) tokens are its candidates.
All inputs are finite; a program needn't handle non-finite values.
Results may differ from a plain program's by a relative error of at most 0.0052.
The roundings to bfloat16 on the way count: a program that leaves them out, or rounds other values in their place, can miss the bound.
Values may be sent and summed in bfloat16 or wider, within the bound.
A program may use at most 64 MiB of HBM per device.

v0:
```python
import math

import jax
import jax.numpy as jnp
from jax import lax
from jax.sharding import PartitionSpec as P

HD = 128
D = 1024
BACK = 3


norm_eps = 1e-06


def passed_along(block, axis, distance):
    devices = range(lax.axis_size(axis))
    route = [(i - distance, i) for i in devices if i - distance in devices]
    return lax.ppermute(block, axis, route)


def user_bounds(positions, user_lengths, cand_counts):
    ends_at = jnp.cumsum(user_lengths)
    starts_at = ends_at - user_lengths
    first_cand = ends_at - jnp.minimum(cand_counts, user_lengths)
    inside = (positions[:, None] >= starts_at[None, :]) & (positions[:, None] < ends_at[None, :])
    seg_start = jnp.sum(jnp.where(inside, starts_at[None, :], 0), axis=1)
    cand_start = jnp.sum(jnp.where(inside, first_cand[None, :], 0), axis=1)
    return (seg_start, cand_start)


def visible(query_pos, key_pos, seg_start, cand_start, reach):
    before = key_pos[None, :] <= query_pos[:, None]
    recent = query_pos[:, None] - key_pos[None, :] < reach
    same_user = key_pos[None, :] >= seg_start[:, None]
    history = (key_pos[None, :] < cand_start[:, None]) | (key_pos[None, :] == query_pos[:, None])
    return before & recent & same_user & history


def silu_slope(scores):
    sigma = jax.nn.sigmoid(scores)
    return sigma * (1.0 + scores * (1.0 - sigma))


def key_window(nearby):
    found = [passed_along(nearby, "ctx", offset) for offset in range(1, BACK + 1)]
    return jnp.concatenate(found[::-1] + [nearby], axis=1)


def key_window_again(nearby):
    found = [passed_along(nearby, "ctx", offset) for offset in range(1, BACK + 1)]
    return jnp.concatenate(found[::-1] + [nearby], axis=1)


def per_device(
    queries, key_rows, value_rows, gating, gain_vector, out_grad, user_lengths, cand_counts
):
    tok_count, feat_count = queries.shape
    head_count = feat_count // HD
    scale = 1.0 / math.sqrt(HD)
    margin = BACK * tok_count
    width = margin + tok_count
    device_first = lax.axis_index("ctx") * tok_count
    query_pos = device_first + jnp.arange(tok_count, dtype=jnp.int32)
    key_pos = device_first - margin + jnp.arange(width, dtype=jnp.int32)
    seg_start, cand_start = user_bounds(query_pos, user_lengths, cand_counts)
    allowed = visible(query_pos, key_pos, seg_start, cand_start, margin).astype(jnp.float32)[None]
    query_heads = queries.reshape(tok_count, head_count, HD)
    nearby = jnp.stack([key_rows, value_rows])

    def attend(window):
        keys_win = window[0].reshape(width, head_count, HD)
        values_win = window[1].reshape(width, head_count, HD)
        scores = (
            jnp.einsum("qhd,khd->hqk", query_heads, keys_win, preferred_element_type=jnp.float32)
            * scale
        )
        attn = (jax.nn.silu(scores) * allowed / margin).astype(jnp.bfloat16)
        return (keys_win, values_win, scores, attn)

    keys_win, values_win, scores, attn = attend(key_window(nearby))
    mixed = jnp.einsum(
        "hqk,khd->qhd", attn, values_win, preferred_element_type=jnp.float32
    ).reshape(tok_count, feat_count)
    gain_f = gain_vector.astype(jnp.float32)
    gate_f = gating.astype(jnp.float32)
    grad_f = out_grad.astype(jnp.float32)
    dnorm = grad_f * gate_f * gain_f
    first_sum, square_sum = lax.psum(
        (jnp.sum(mixed, axis=1), jnp.sum(mixed * mixed, axis=1)), "head"
    )
    row_mean = first_sum / D
    row_var = square_sum / D - row_mean * row_mean
    rstd = lax.rsqrt(row_var + norm_eps)
    normed = (mixed - row_mean[:, None]) * rstd[:, None]
    sum_one, sum_two = lax.psum((jnp.sum(dnorm, axis=1), jnp.sum(dnorm * normed, axis=1)), "head")
    mean_one = sum_one / D
    mean_two = sum_two / D
    output = (normed * gain_f * gate_f).astype(jnp.bfloat16)
    gate_grad = (grad_f * normed * gain_f).astype(jnp.bfloat16)
    dmixed = (rstd[:, None] * (dnorm - mean_one[:, None] - normed * mean_two[:, None])).astype(
        jnp.bfloat16
    )
    dmixed_heads = dmixed.reshape(tok_count, head_count, HD)
    back_keys, back_values, back_scores, back_attn = attend(key_window_again(nearby))
    dattn = jnp.einsum(
        "qhd,khd->hqk", dmixed_heads, back_values, preferred_element_type=jnp.float32
    )
    dv_win = jnp.einsum("hqk,qhd->khd", back_attn, dmixed_heads, preferred_element_type=jnp.float32)
    dscore = (dattn * silu_slope(back_scores) * allowed / margin).astype(jnp.bfloat16)
    query_grad = (
        (jnp.einsum("hqk,khd->qhd", dscore, back_keys, preferred_element_type=jnp.float32) * scale)
        .reshape(tok_count, feat_count)
        .astype(jnp.bfloat16)
    )
    dk_win = (
        jnp.einsum("hqk,qhd->khd", dscore, query_heads, preferred_element_type=jnp.float32) * scale
    )
    grad_terms = jnp.stack([dk_win.reshape(width, feat_count), dv_win.reshape(width, feat_count)])
    received = jnp.zeros((2, tok_count, feat_count), jnp.float32)
    for offset in range(1, BACK + 1):
        piece = grad_terms[:, (BACK - offset) * tok_count : (BACK - offset + 1) * tok_count]
        received = received + passed_along(piece, "ctx", -offset)
    own_terms = grad_terms[:, margin:] + received
    key_grad = own_terms[0].astype(jnp.bfloat16)
    value_grad = own_terms[1].astype(jnp.bfloat16)
    return (output, query_grad, key_grad, value_grad, gate_grad)


def solution(mesh):
    placed = (
        P("ctx", "head"),
        P("ctx", "head"),
        P("ctx", "head"),
        P("ctx", "head"),
        P("head"),
        P("ctx", "head"),
        P(),
        P(),
    )
    return jax.shard_map(
        per_device,
        mesh=mesh,
        in_specs=placed,
        out_specs=(
            P("ctx", "head"),
            P("ctx", "head"),
            P("ctx", "head"),
            P("ctx", "head"),
            P("ctx", "head"),
        ),
        check_vma=False,
    )
```

profile of v0, /device:TPU:186, one launch (start us, length us, event | category | flops | bytes accessed | tf_op | source)
XLA Modules:
  0.0 218.3 jit_solution(10610858646007088428)
XLA Ops:
  0.6 1.1 copy.46
  1.7 1.1 copy.47
  2.8 0.1 pad_maximum_fusion.1
  2.9 6.6 %collective-permute-start = (bf16[2,512,256]{1,2,0:T(8,128)(2,1)S(1)}, bf16[2,512,256]{1,2,0:T(8,128)(2,1)S(1)}, u32[]{:S(2)}, u32[]{:S(2)}) collective-permute-start(bf16[2,512,256]{1,2,0:T(8,128)(2,1)S(1)} %pad_maximum_fusion.1), channel_id=1, source_target_pairs={{0,12},{4,16},{8,20},{12,24},{16,28},{20,32},{24,36},{28,40},{32,4... | collective-permute-start | bytes 1572872 | tf_op jit(solution)/shard_map/ppermute | solution.py:19
  9.5 4.3 %collective-permute-start.1 = (bf16[2,512,256]{1,2,0:T(8,128)(2,1)S(1)}, bf16[2,512,256]{1,2,0:T(8,128)(2,1)S(1)}, u32[]{:S(2)}, u32[]{:S(2)}) collective-permute-start(bf16[2,512,256]{1,2,0:T(8,128)(2,1)S(1)} %pad_maximum_fusion.1), channel_id=1, source_target_pairs={{0,8},{4,12},{8,16},{12,20},{16,24},{20,28},{24,32},{28,36},{32,40... | collective-permute-start | bytes 1572872 | tf_op jit(solution)/shard_map/ppermute | solution.py:19
  13.8 3.7 %collective-permute-start.2 = (bf16[2,512,256]{1,2,0:T(8,128)(2,1)S(1)}, bf16[2,512,256]{1,2,0:T(8,128)(2,1)S(1)}, u32[]{:S(2)}, u32[]{:S(2)}) collective-permute-start(bf16[2,512,256]{1,2,0:T(8,128)(2,1)S(1)} %pad_maximum_fusion.1), channel_id=1, source_target_pairs={{0,4},{4,8},{8,12},{12,16},{16,20},{20,24},{24,28},{28,32},{32,36}... | collective-permute-start | bytes 1572872 | tf_op jit(solution)/shard_map/ppermute | solution.py:19
  17.6 1.1 copy.70
  18.7 0.0 copy-start.6
  18.7 0.7 convert_element_type.51
  19.4 0.8 reduce-window.8
  20.2 0.7 minimum_subtract_fusion
  20.9 0.1 select_reduce_fusion.1
  21.0 1.4 fusion.15
  22.4 0.0 copy-start.3
  22.4 0.0 collective-permute-done
  22.4 10.2 %collective-permute-done.1 = bf16[2,512,256]{1,2,0:T(8,128)(2,1)S(1)} collective-permute-done((bf16[2,512,256]{1,2,0:T(8,128)(2,1)S(1)}, bf16[2,512,256]{1,2,0:T(8,128)(2,1)S(1)}, u32[]{:S(2)}, u32[]{:S(2)}) %collective-permute-start.1) | collective-permute-done | bytes 524320 | tf_op jit(solution)/shard_map/ppermute | solution.py:19
  32.7 4.9 %collective-permute-done.2 = bf16[2,512,256]{1,2,0:T(8,128)(2,1)S(1)} collective-permute-done((bf16[2,512,256]{1,2,0:T(8,128)(2,1)S(1)}, bf16[2,512,256]{1,2,0:T(8,128)(2,1)S(1)}, u32[]{:S(2)}, u32[]{:S(2)}) %collective-permute-start.2) | collective-permute-done | bytes 524320 | tf_op jit(solution)/shard_map/ppermute | solution.py:19
  37.6 0.3 maximum_maximum_fusion
  37.9 0.1 fusion.28
  38.0 0.0 copy-start.4
  38.1 5.5 %fusion.5 = (bf16[2,512,2048]{1,2,0:T(8,128)(2,1)S(1)}, f32[2,2048,512]{2,1,0:T(8,128)}) fusion(f32[512,2048]{0,1:T(8,128)S(1)} %fusion.15, bf16[2048,2,128]{0,2,1:T(8,128)(2,1)S(1)} %bitcast.76, bf16[512,2,128]{0,2,1:T(8,128)(2,1)S(1)} %bitcast.84), kind=kOutput, calls=%fused_computation.8 | convolution fusion | flops 553648128 | bytes 18087936 | tf_op jit(solution)/shard_map/qhd,khd->hqk/dot_general | solution.py:75
  43.6 1.9 copy-done
  45.5 0.8 fusion.26
  46.3 0.1 reduce_sum.56
  46.4 0.2 copy.51
  46.6 9.7 %all-reduce.1 = (f32[512]{0:T(512)S(1)}, f32[512]{0:T(512)S(1)}) all-reduce(f32[512]{0:T(512)S(1)} %get-tuple-element.44, f32[512]{0:T(512)S(1)} %reduce_sum.56), channel_id=1, replica_groups=mesh['ctx'=128,'head'=4] {'head'}, use_global_device_ids=true, to_apply=%region_6.7 | all-reduce | flops 1024 | bytes 8192 | tf_op jit(solution)/shard_map/psum | solution.py:89
  56.3 1.3 fusion.27
  57.6 9.6 %all-reduce = (f32[512]{0:T(512)S(1)}, f32[512]{0:T(512)S(1)}) all-reduce(f32[512]{0:T(512)S(1)} %get-tuple-element.21, f32[512]{0:T(512)S(1)} %get-tuple-element.20), channel_id=1, replica_groups=mesh['ctx'=128,'head'=4] {'head'}, use_global_device_ids=true, to_apply=%region_10.11 | all-reduce | flops 1024 | bytes 8192 | tf_op jit(solution)/shard_map/psum | solution.py:96
  67.2 2.1 fusion.25
  69.3 0.1 copy.71
  69.4 5.0 %fusion.29 = f32[2,128,2048]{2,1,0:T(8,128)} fusion(bf16[512,2,128]{0,2,1:T(8,128)(2,1)S(1)} %bitcast.86, bf16[2,512,2048]{1,2,0:T(8,128)(2,1)} %copy-done), kind=kOutput, calls=%fused_computation.64 | convolution fusion | flops 536870912 | bytes 6553600 | tf_op jit(solution)/shard_map/hqk,qhd->khd/dot_general | solution.py:109
  74.4 1.9 copy.61
  76.4 0.0 copy-start.7
  76.4 7.5 %fusion.11 = bf16[2,512,2048]{1,2,0:T(8,128)(2,1)S(1)} fusion(f32[2,2048,512]{2,1,0:T(8,128)} %get-tuple-element.43, bf16[512,2,128]{0,2,1:T(8,128)(2,1)S(1)} %bitcast.87, bf16[2048,2,128]{0,2,1:T(8,128)(2,1)} %bitcast.79, f32[512,2048]{0,1:T(8,128)} %copy-done.3), kind=kOutput, calls=%fused_computation.14 | convolution fusion | flops 562036736 | bytes 18087936 | tf_op jit(solution)/shard_map/qhd,khd->hqk/dot_general | solution.py:106
  83.9 1.9 copy-done.1
  85.8 2.8 %convolution_multiply_fusion = f32[2,2048,128]{1,2,0:T(8,128)} fusion(bf16[2,512,2048]{1,2,0:T(8,128)(2,1)S(1)} %fusion.11, bf16[512,2,128]{0,2,1:T(8,128)(2,1)S(1)} %bitcast.85), kind=kOutput, calls=%fused_computation.26 | convolution fusion | flops 537395200 | bytes 6553600 | tf_op jit(solution)/shard_map/hqk,qhd->khd/dot_general | solution.py:117
  88.6 2.9 %copy.60 = f32[1,2048,256]{2,1,0:T(8,128)} copy(f32[1,2048,256]{1,2,0:T(8,128)} %bitcast.74) | data formatting | bytes 4194304 | tf_op jit(solution)/shard_map/stack;reshape | solution.py:119
  91.5 3.2 %fusion.17 = (f32[2,512,256]{2,1,0:T(8,128)}, f32[2,512,256]{2,1,0:T(8,128)}, f32[2,512,256]{2,1,0:T(8,128)}) fusion(f32[1,2048,256]{2,1,0:T(8,128)} %copy.60, f32[1,2048,256]{2,1,0:T(8,128)S(1)} %copy.61), kind=kLoop, calls=%fused_computation.30 | loop fusion | flops 786432 | bytes 7340032 | tf_op jit(solution)/shard_map/stack | solution.py:119
  94.8 10.4 %collective-permute-start.3 = (f32[2,512,256]{2,1,0:T(8,128)}, f32[2,512,256]{2,1,0:T(8,128)}, u32[]{:S(2)}, u32[]{:S(2)}) collective-permute-start(f32[2,512,256]{2,1,0:T(8,128)} %get-tuple-element.29), channel_id=1, source_target_pairs={{4,0},{8,4},{12,8},{16,12},{20,16},{24,20},{28,24},{32,28},{36,32}... | collective-permute-start | bytes 3145736 | tf_op jit(solution)/shard_map/ppermute | solution.py:19
  105.2 1.9 collective-permute-start.4
  107.1 3.3 %collective-permute-start.5 = (f32[2,512,256]{2,1,0:T(8,128)}, f32[2,512,256]{2,1,0:T(8,128)}, u32[]{:S(2)}, u32[]{:S(2)}) collective-permute-start(f32[2,512,256]{2,1,0:T(8,128)} %get-tuple-element.30), channel_id=1, source_target_pairs={{12,0},{16,4},{20,8},{24,12},{28,16},{32,20},{36,24},{40,28},{44,3... | collective-permute-start | bytes 3145736 | tf_op jit(solution)/shard_map/ppermute | solution.py:19
  110.4 0.7 fusion.16
  111.1 0.8 copy.62
  112.0 32.0 %collective-permute-done.3 = f32[2,512,256]{2,1,0:T(8,128)} collective-permute-done((f32[2,512,256]{2,1,0:T(8,128)}, f32[2,512,256]{2,1,0:T(8,128)}, u32[]{:S(2)}, u32[]{:S(2)}) %collective-permute-start.3) | collective-permute-done | bytes 1048608 | tf_op jit(solution)/shard_map/ppermute | solution.py:19
  143.9 6.6 %collective-permute-done.4 = f32[2,512,256]{2,1,0:T(8,128)} collective-permute-done((f32[2,512,256]{2,1,0:T(8,128)}, f32[2,512,256]{2,1,0:T(8,128)}, u32[]{:S(2)}, u32[]{:S(2)}) %collective-permute-start.4) | collective-permute-done | bytes 1048608 | tf_op jit(solution)/shard_map/ppermute | solution.py:19
  150.6 64.7 %collective-permute-done.5 = f32[2,512,256]{2,1,0:T(8,128)} collective-permute-done((f32[2,512,256]{2,1,0:T(8,128)}, f32[2,512,256]{2,1,0:T(8,128)}, u32[]{:S(2)}, u32[]{:S(2)}) %collective-permute-start.5) | collective-permute-done | bytes 1048608 | tf_op jit(solution)/shard_map/ppermute | solution.py:19
  215.3 2.2 %fusion.20 = bf16[2,512,256]{2,1,0:T(8,128)(2,1)S(1)} fusion(f32[1,2048,256]{2,1,0:T(8,128)} %copy.60, f32[1,2048,256]{2,1,0:T(8,128)S(1)} %copy.61, f32[2,512,256]{2,1,0:T(8,128)} %collective-permute-done.5, f32[2,512,256]{2,1,0:T(8,128)} %collective-permute-done.3, f32[2,512,256]{2,1,0:T(8,128)} %collective-permute-done.4), kind=kLoop, calls=%fused_computation.33 | loop fusion | flops 1310720 | bytes 7864320 | tf_op jit(solution)/shard_map/convert.1
  217.5 0.8 slice_bitcast_fusion
  (14 shorter events, 0.0 us)
Async XLA Ops:
  2.9 19.5 %collective-permute-start = (bf16[2,512,256]{1,2,0:T(8,128)(2,1)S(1)}, bf16[2,512,256]{1,2,0:T(8,128)(2,1)S(1)}, u32[]{:S(2)}, u32[]{:S(2)}) collective-permute-start(bf16[2,512,256]{1,2,0:T(8,128)(2,1)S(1)} %pad_maximum_fusion.1), channel_id=1, source_target_pairs={{0,12},{4,16},{8,20},{12,24},{16,28},{20,32},{24,36},{28,40},{32,4... | collective-permute-start | bytes 1572872 | tf_op jit(solution)/shard_map/ppermute | solution.py:19
  9.5 23.1 %collective-permute-start.1 = (bf16[2,512,256]{1,2,0:T(8,128)(2,1)S(1)}, bf16[2,512,256]{1,2,0:T(8,128)(2,1)S(1)}, u32[]{:S(2)}, u32[]{:S(2)}) collective-permute-start(bf16[2,512,256]{1,2,0:T(8,128)(2,1)S(1)} %pad_maximum_fusion.1), channel_id=1, source_target_pairs={{0,8},{4,12},{8,16},{12,20},{16,24},{20,28},{24,32},{28,36},{32,40... | collective-permute-start | bytes 1572872 | tf_op jit(solution)/shard_map/ppermute | solution.py:19
  13.8 23.8 %collective-permute-start.2 = (bf16[2,512,256]{1,2,0:T(8,128)(2,1)S(1)}, bf16[2,512,256]{1,2,0:T(8,128)(2,1)S(1)}, u32[]{:S(2)}, u32[]{:S(2)}) collective-permute-start(bf16[2,512,256]{1,2,0:T(8,128)(2,1)S(1)} %pad_maximum_fusion.1), channel_id=1, source_target_pairs={{0,4},{4,8},{8,12},{12,16},{16,20},{20,24},{24,28},{28,32},{32,36}... | collective-permute-start | bytes 1572872 | tf_op jit(solution)/shard_map/ppermute | solution.py:19
  18.7 19.3 %copy-start.6 = (bf16[512,256]{0,1:T(8,128)(2,1)}, bf16[512,256]{0,1:T(8,128)(2,1)S(1)}, u32[]{:S(2)}) copy-start(bf16[512,256]{0,1:T(8,128)(2,1)S(1)} %copy.70) | copy-start | bytes 786436
  22.4 15.6 %copy-start.3 = (f32[512,2048]{0,1:T(8,128)}, f32[512,2048]{0,1:T(8,128)S(1)}, u32[]{:S(2)}) copy-start(f32[512,2048]{0,1:T(8,128)S(1)} %fusion.15) | copy-start | bytes 12582916
  38.0 5.6 %copy-start.4 = (bf16[1,2048,256]{1,2,0:T(8,128)(2,1)}, bf16[1,2048,256]{1,2,0:T(8,128)(2,1)S(1)}, u32[]{:S(2)}) copy-start(bf16[1,2048,256]{1,2,0:T(8,128)(2,1)S(1)} %get-tuple-element.32) | copy-start | bytes 3145732
  43.6 2.0 copy-start
  43.6 12.7 %copy-start.5 = (bf16[512,256]{1,0:T(8,128)(2,1)S(1)}, bf16[512,256]{1,0:T(8,128)(2,1)}, u32[]{:S(2)}) copy-start(bf16[512,256]{1,0:T(8,128)(2,1)} %param.13) | copy-start | bytes 786436
  76.4 9.5 %copy-start.7 = (bf16[512,256]{0,1:T(8,128)(2,1)S(1)}, bf16[512,256]{0,1:T(8,128)(2,1)}, u32[]{:S(2)}) copy-start(bf16[512,256]{0,1:T(8,128)(2,1)} %copy-done.6) | copy-start | bytes 786436
  83.9 1.9 copy-start.1
  91.5 18.9 %copy-start.2 = (bf16[2,512,2048]{1,2,0:T(8,128)(2,1)S(1)}, bf16[2,512,2048]{1,2,0:T(8,128)(2,1)}, u32[]{:S(2)}) copy-start(bf16[2,512,2048]{1,2,0:T(8,128)(2,1)} %copy-done.1) | copy-start | bytes 12582916
  94.8 49.2 %collective-permute-start.3 = (f32[2,512,256]{2,1,0:T(8,128)}, f32[2,512,256]{2,1,0:T(8,128)}, u32[]{:S(2)}, u32[]{:S(2)}) collective-permute-start(f32[2,512,256]{2,1,0:T(8,128)} %get-tuple-element.29), channel_id=1, source_target_pairs={{4,0},{8,4},{12,8},{16,12},{20,16},{24,20},{28,24},{32,28},{36,32}... | collective-permute-start | bytes 3145736 | tf_op jit(solution)/shard_map/ppermute | solution.py:19
  105.2 45.4 %collective-permute-start.4 = (f32[2,512,256]{2,1,0:T(8,128)}, f32[2,512,256]{2,1,0:T(8,128)}, u32[]{:S(2)}, u32[]{:S(2)}) collective-permute-start(f32[2,512,256]{2,1,0:T(8,128)} %get-tuple-element.28), channel_id=1, source_target_pairs={{8,0},{12,4},{16,8},{20,12},{24,16},{28,20},{32,24},{36,28},{40,32... | collective-permute-start | bytes 3145736 | tf_op jit(solution)/shard_map/ppermute | solution.py:19
  107.1 108.1 %collective-permute-start.5 = (f32[2,512,256]{2,1,0:T(8,128)}, f32[2,512,256]{2,1,0:T(8,128)}, u32[]{:S(2)}, u32[]{:S(2)}) collective-permute-start(f32[2,512,256]{2,1,0:T(8,128)} %get-tuple-element.30), channel_id=1, source_target_pairs={{12,0},{16,4},{20,8},{24,12},{28,16},{32,20},{36,24},{40,28},{44,3... | collective-permute-start | bytes 3145736 | tf_op jit(solution)/shard_map/ppermute | solution.py:19
where the time goes:
time: 219 us; the launch traced here: 218 us
  waiting for transfers between devices  118 us (54%)
  starting transfers between devices  30.3 us (14%)
  matrix products  22.4 us (10%)
  blocking collectives  19.3 us (9%)
  local copies, waits for them, and re-layouts  14.2 us (6%)
  other arithmetic  13 us (6%)
    ppermute x6, waiting for transfers between devices, passed_along(): return lax.ppermute(block, axis, route)  118 us
    ppermute x6, starting transfers between devices, passed_along(): return lax.ppermute(block, axis, route)  30.3 us
    psum x1, blocking collectives, per_device(): lax.psum((jnp.sum(mixed, axis=1), jnp.sum(mixed * mixed, axis=1)), 'head')  9.68 us
    psum x1, blocking collectives, per_device(): lax.psum((jnp.sum(dnorm, axis=1), jnp.sum(dnorm * normed, axis=1)), 'head')  9.58 us
    dot_general x1, matrix products, per_device(): jnp.einsum('qhd,khd->hqk', dmixed_heads, back_values, preferred_element_t...  7.49 us
    unnamed x19, local copies, waits for them, and re-layouts  6.93 us
    dot_general x1, matrix products, attend(): jnp.einsum('qhd,khd->hqk', query_heads, keys_win, preferred_element_type=...  5.54 us
    dot_general x1, matrix products, per_device(): jnp.einsum('hqk,qhd->khd', back_attn, dmixed_heads, preferred_element_typ...  5.01 us
  transfers between devices with their start and end apart: 6, of which 5 were waited for; matrix products, arithmetic and copies ran while one was open for 3% of the time, Pallas kernels for 0%

commit v1 on v0

v1 whole, which is shorter than its diff:
```python
import functools
import math

import jax
import jax.numpy as jnp
from jax import lax
from jax.experimental import pallas as pl
from jax.experimental.pallas import tpu as pltpu
from jax.sharding import PartitionSpec as P

HD = 128
D = 1024
T = 512
HALF = 256
BACK = 3
WINDOW = 1536
USERS = 4
NC = 4
CH = T // NC
EPS = 1e-06
SCALE = 1.0 / math.sqrt(HD)
MESH = pl.DeviceIdType.MESH
NT = (((1,), (1,)), ((), ()))
NN = (((1,), (0,)), ((), ()))
TN = (((0,), (0,)), ((), ()))
F32 = jnp.float32
BF16 = jnp.bfloat16


def dot(a, b, dims):
    return lax.dot_general(a, b, dims, preferred_element_type=F32)


def dot_exact(a, b, dims):
    return lax.dot_general(a, b, dims, preferred_element_type=F32, precision=lax.Precision.HIGHEST)


def query_bounds(pos, lengths, cands):
    seg = jnp.zeros_like(pos)
    cand = jnp.zeros_like(pos)
    start = jnp.int32(0)
    for u in range(USERS):
        length = lengths[u]
        end = start + length
        first = end - jnp.minimum(cands[u], length)
        inside = (pos >= start) & (pos < end)
        seg = jnp.where(inside, start, seg)
        cand = jnp.where(inside, first, cand)
        start = end
    return jnp.maximum(seg, pos - (WINDOW - 1)), jnp.minimum(cand, pos)


def weights(prod, allowed):
    h = prod * (0.5 * SCALE)
    w = 1.0 + jnp.tanh(h)
    a = jnp.where(allowed, w * (1.0 / WINDOW), 0.0)
    attn = (h * a).astype(BF16)
    slope = a * (0.5 + h * (1.0 - 0.5 * w))
    return attn, slope


def spans_q(d):
    if d == 0:
        return ((0, 0, HALF), (1, 0, T))
    if d == BACK:
        return ((0, 0, T), (1, HALF, HALF))
    return ((0, 0, T), (1, 0, T))


def spans_k(d):
    if d == 0:
        return ((0, 0, T), (1, HALF, HALF))
    if d == BACK:
        return ((0, 0, HALF), (1, 0, T))
    return ((0, 0, T), (1, 0, T))


def kernel(
    len_ref, cand_ref, gain_ref, q_hbm, k_hbm, v_hbm, gate_hbm, og_hbm,
    out_ref, dq_ref, dk_ref, dv_ref, dgate_ref,
    kbuf, vbuf, qbuf, dbuf, pk, pv, pq, pd, gate, og, mixed, dkacc, dvacc,
    slope_q, attn_k, slope_k, lo_q, hi_q, lo_k, hi_k, stats,
    loc, kvy_s, kvy_r, kvx_s, kvx_r, qy_s, qy_r, qx_s, qx_r, dy_s, dy_r, dx_s, dx_r, st_s, st_r,
):
    c = lax.axis_index("ctx")
    hd = lax.axis_index("head")
    x = lax.rem(c, 4)
    row0 = c - x
    nctx = 128

    def row_peer(d):
        return {"ctx": row0 + lax.rem(x + d + 4, 4), "head": hd}

    def ctx_peer(d):
        return {"ctx": lax.rem(c + d + nctx, nctx), "head": hd}

    def head_peer(e):
        return {"ctx": c, "head": lax.rem(hd + e, 4)}

    bar = pltpu.get_barrier_semaphore()
    peers = [row_peer(1), row_peer(2), row_peer(3), ctx_peer(4), ctx_peer(-4)]
    peers += [head_peer(1), head_peer(2), head_peer(3)]
    for p in peers:
        pl.semaphore_signal(bar, inc=1, device_id=p, device_id_type=MESH)

    loads = [
        pltpu.make_async_copy(src, dst, loc.at[i])
        for i, (src, dst) in enumerate(
            ((q_hbm, qbuf.at[0]), (k_hbm, kbuf.at[0]), (v_hbm, vbuf.at[0]), (gate_hbm, gate), (og_hbm, og))
        )
    ]
    for cp in loads:
        cp.start()
    pl.semaphore_wait(bar, len(peers))

    def rows(ch):
        return pl.ds(ch * CH, CH)

    def remote(src, dst, ss, rs, dev):
        return pltpu.make_async_remote_copy(src, dst, ss, rs, device_id=dev, device_id_type=MESH)

    def kv_y(a, ch):
        src, dst = ((k_hbm, pk), (v_hbm, pv))[a]
        return remote(src.at[rows(ch)], dst.at[rows(ch)], kvy_s.at[a, ch], kvy_r.at[a, ch], ctx_peer(4))

    def kv_x(a, d, ch, own):
        src = ((k_hbm, v_hbm) if own else (pk, pv))[a]
        dst = (kbuf, vbuf)[a]
        return remote(
            src.at[rows(ch)], dst.at[d, rows(ch)], kvx_s.at[a, d - 1, ch], kvx_r.at[a, d - 1, ch], row_peer(d)
        )

    def q_y(ch):
        return remote(q_hbm.at[rows(ch)], pq.at[rows(ch)], qy_s.at[ch], qy_r.at[ch], ctx_peer(-4))

    def q_x(d, ch, own):
        src = q_hbm if own else pq
        return remote(src.at[rows(ch)], qbuf.at[d, rows(ch)], qx_s.at[d - 1, ch], qx_r.at[d - 1, ch], row_peer(-d))

    def d_y(ch):
        return remote(dbuf.at[0, rows(ch)], pd.at[rows(ch)], dy_s.at[ch], dy_r.at[ch], ctx_peer(-4))

    def d_x(d, ch, own):
        src = dbuf.at[0, rows(ch)] if own else pd.at[rows(ch)]
        return remote(src, dbuf.at[d, rows(ch)], dx_s.at[d - 1, ch], dx_r.at[d - 1, ch], row_peer(-d))

    def st(e):
        return remote(stats.at[0], stats.at[e], st_s.at[e - 1], st_r.at[e - 1], head_peer(e))

    @pl.when(x >= 1)
    def _():
        for ch in range(NC):
            for a in range(2):
                kv_y(a, ch).start()

    for d in range(1, BACK + 1):

        @pl.when(x + d < 4)
        def _():
            for ch in range(NC):
                for a in range(2):
                    kv_x(a, d, ch, True).start()

    def fill_rows(t, _):
        r = pl.ds(pl.multiple_of(t * HALF, HALF), HALF)
        pos = c * T + t * HALF + lax.broadcasted_iota(jnp.int32, (HALF, HD), 0)
        lo_q[r, :], hi_q[r, :] = query_bounds(pos, len_ref, cand_ref)
        return 0

    lax.fori_loop(0, 2, fill_rows, 0)
    for d in range(BACK + 1):
        pos = (c + d) * T + lax.broadcasted_iota(jnp.int32, (8, T), 1)
        lo_k[d], hi_k[d] = query_bounds(pos, len_ref, cand_ref)

    mixed[...] = jnp.zeros_like(mixed)
    dkacc[...] = jnp.zeros_like(dkacc)
    dvacc[...] = jnp.zeros_like(dvacc)
    for cp in loads:
        cp.wait()

    def cols(h):
        return pl.ds(pl.multiple_of(h * HD, HD), HD)

    def forward(d):
        def body(h, _):
            hs = cols(h)
            for t, k0, kn in spans_q(d):
                r = pl.ds(t * HALF, HALF)
                prod = dot(qbuf[0, r, hs], kbuf[d, pl.ds(k0, kn), hs], NT)
                key = (c - d) * T + k0 + lax.broadcasted_iota(jnp.int32, (HALF, kn), 1)
                lo = jnp.concatenate([lo_q[r, :]] * (kn // HD), axis=1)
                hi = jnp.concatenate([hi_q[r, :]] * (kn // HD), axis=1)
                allowed = (key >= lo) & (key < hi)
                if d == 0:
                    allowed = allowed | (key == c * T + t * HALF + lax.broadcasted_iota(jnp.int32, (HALF, kn), 0))
                attn, slope = weights(prod, allowed)
                slope_q[h, r, pl.ds(d * T + k0, kn)] = slope
                mixed[r, hs] += dot(attn, vbuf[d, pl.ds(k0, kn), hs], NN)
            return 0

        lax.fori_loop(0, 2, body, 0)

    def keys_before(d):
        def body(h, _):
            hs = cols(h)
            for t, q0, qn in spans_k(d):
                r = pl.ds(t * HALF, HALF)
                prod = dot(kbuf[0, r, hs], qbuf[d, pl.ds(q0, qn), hs], NT)
                key = c * T + t * HALF + lax.broadcasted_iota(jnp.int32, (HALF, qn), 0)
                allowed = (key >= lo_k[d, 0:1, pl.ds(q0, qn)]) & (key < hi_k[d, 0:1, pl.ds(q0, qn)])
                if d == 0:
                    allowed = allowed | (key == c * T + q0 + lax.broadcasted_iota(jnp.int32, (HALF, qn), 1))
                attn, slope = weights(prod, allowed)
                attn_k[h, r, pl.ds(d * T + q0, qn)] = attn
                slope_k[h, r, pl.ds(d * T + q0, qn)] = slope
            return 0

        lax.fori_loop(0, 2, body, 0)

    def keys_after(d):
        def body(h, _):
            hs = cols(h)
            for t, q0, qn in spans_k(d):
                r = pl.ds(t * HALF, HALF)
                dm = dbuf[d, pl.ds(q0, qn), hs]
                dvacc[r, hs] += dot(attn_k[h, r, pl.ds(d * T + q0, qn)], dm, NN)
                dattn = dot(vbuf[0, r, hs], dm, NT)
                dscore = (dattn * slope_k[h, r, pl.ds(d * T + q0, qn)]).astype(BF16)
                dkacc[r, hs] += dot(dscore, qbuf[d, pl.ds(q0, qn), hs], NN)
            return 0

        lax.fori_loop(0, 2, body, 0)

    def query_grad(h, _):
        hs = cols(h)
        for t in range(2):
            r = pl.ds(t * HALF, HALF)
            dm = dbuf[0, r, hs]
            total = jnp.zeros((HALF, HD), F32)
            for d in range(BACK + 1):
                _, k0, kn = spans_q(d)[t]
                dattn = dot(dm, vbuf[d, pl.ds(k0, kn), hs], NT)
                dscore = (dattn * slope_q[h, r, pl.ds(d * T + k0, kn)]).astype(BF16)
                total += dot(dscore, kbuf[d, pl.ds(k0, kn), hs], NN)
            dq_ref[r, hs] = (total * SCALE).astype(BF16)
        return 0

    forward(0)

    @pl.when(x >= 1)
    def _():
        for ch in range(NC):
            for a in range(2):
                kv_y(a, ch).wait_recv()
                for d in range(1, BACK + 1):

                    @pl.when(x + d >= 4)
                    def _():
                        kv_x(a, d, ch, False).start()

    def wait_kv(d):
        for ch in range(NC):
            for a in range(2):
                kv_x(a, d, ch, True).wait_recv()

    wait_kv(1)
    forward(1)

    @pl.when(x <= 2)
    def _():
        for ch in range(NC):
            q_y(ch).start()

    wait_kv(2)
    forward(2)
    wait_kv(3)
    for d in range(1, BACK + 1):

        @pl.when(x - d >= 0)
        def _():
            for ch in range(NC):
                q_x(d, ch, True).start()

    forward(3)

    gain = gain_ref[...].astype(F32)
    pick = lax.broadcasted_iota(jnp.int32, (8, HD), 0)

    def fold(a):
        return a[:, :HD] + a[:, HD:]

    m = mixed[...]
    dnorm = og[...].astype(F32) * gate[...].astype(F32) * gain
    total = jnp.zeros((8, T), F32)
    for i, a in enumerate((m, m * m, dnorm, dnorm * m)):
        total += dot_exact((pick == i).astype(F32), fold(a), NT)
    stats[0] = total
    for e in range(1, 4):
        st(e).start()

    @pl.when(x <= 2)
    def _():
        for ch in range(NC):
            q_y(ch).wait_recv()
            for d in range(1, BACK + 1):

                @pl.when(x - d < 0)
                def _():
                    q_x(d, ch, False).start()

    keys_before(0)
    for e in range(1, 4):
        st(e).wait_recv()
    total = stats[0] + stats[1] + stats[2] + stats[3]
    mean = total[0:1] / D
    var = total[1:2] / D - mean * mean
    rstd = lax.rsqrt(var + EPS)
    mean_one = total[2:3] / D
    mean_two = rstd * (total[3:4] - mean * total[2:3]) / D
    coef = jnp.concatenate([mean, rstd, mean_one, mean_two, jnp.zeros((4, T), F32)], axis=0)
    wide = []
    for i in range(4):
        b = dot_exact(coef, (pick == i).astype(F32), TN)
        wide.append(jnp.concatenate([b, b], axis=1))
    mean, rstd, mean_one, mean_two = wide
    normed = (mixed[...] - mean) * rstd
    gf = gate[...].astype(F32)
    of = og[...].astype(F32)
    dbuf[0] = (rstd * (of * gf * gain - mean_one - normed * mean_two)).astype(BF16)

    @pl.when(x <= 2)
    def _():
        for ch in range(NC):
            d_y(ch).start()

    for d in range(1, BACK + 1):

        @pl.when(x - d >= 0)
        def _():
            for ch in range(NC):
                d_x(d, ch, True).start()

    out_ref[...] = (normed * gain * gf).astype(BF16)
    dgate_ref[...] = (of * normed * gain).astype(BF16)

    query_grad(0, 0)

    @pl.when(x <= 2)
    def _():
        for ch in range(NC):
            d_y(ch).wait_recv()
            for d in range(1, BACK + 1):

                @pl.when(x - d < 0)
                def _():
                    d_x(d, ch, False).start()

    query_grad(1, 0)
    keys_after(0)
    for d in range(1, BACK + 1):
        for ch in range(NC):
            q_x(d, ch, True).wait_recv()
        keys_before(d)
    for d in range(1, BACK + 1):
        for ch in range(NC):
            d_x(d, ch, True).wait_recv()
        keys_after(d)
    dk_ref[...] = (dkacc[...] * SCALE).astype(BF16)
    dv_ref[...] = dvacc[...].astype(BF16)

    @pl.when(x >= 1)
    def _():
        for ch in range(NC):
            for a in range(2):
                kv_y(a, ch).wait_send()

    @pl.when(x <= 2)
    def _():
        for ch in range(NC):
            q_y(ch).wait_send()
            d_y(ch).wait_send()

    for d in range(1, BACK + 1):
        st(d).wait_send()
        for ch in range(NC):
            for a in range(2):
                kv_x(a, d, ch, True).wait_send()
            q_x(d, ch, True).wait_send()
            d_x(d, ch, True).wait_send()


def per_device(queries, key_rows, value_rows, gating, gain_vector, out_grad, user_lengths, cand_counts):
    feat = queries.shape[1]
    block = jax.ShapeDtypeStruct((T, feat), BF16)
    vmem = pl.BlockSpec(memory_space=pltpu.VMEM)
    smem = pl.BlockSpec(memory_space=pltpu.SMEM)
    hbm = pl.BlockSpec(memory_space=pl.ANY)
    sem = pltpu.SemaphoreType.DMA
    output, query_grad, key_grad, value_grad, gate_grad = pl.pallas_call(
        kernel,
        out_shape=[block] * 5,
        in_specs=[smem, smem, vmem, hbm, hbm, hbm, hbm, hbm],
        out_specs=[vmem] * 5,
        scratch_shapes=[
            pltpu.VMEM((4, T, feat), BF16),
            pltpu.VMEM((4, T, feat), BF16),
            pltpu.VMEM((4, T, feat), BF16),
            pltpu.VMEM((4, T, feat), BF16),
            pltpu.VMEM((T, feat), BF16),
            pltpu.VMEM((T, feat), BF16),
            pltpu.VMEM((T, feat), BF16),
            pltpu.VMEM((T, feat), BF16),
            pltpu.VMEM((T, feat), BF16),
            pltpu.VMEM((T, feat), BF16),
            pltpu.VMEM((T, feat), F32),
            pltpu.VMEM((T, feat), F32),
            pltpu.VMEM((T, feat), F32),
            pltpu.VMEM((2, T, 4 * T), F32),
            pltpu.VMEM((2, T, 4 * T), BF16),
            pltpu.VMEM((2, T, 4 * T), F32),
            pltpu.VMEM((T, HD), jnp.int32),
            pltpu.VMEM((T, HD), jnp.int32),
            pltpu.VMEM((4, 8, T), jnp.int32),
            pltpu.VMEM((4, 8, T), jnp.int32),
            pltpu.VMEM((4, 8, T), F32),
            sem((5,)),
            sem((2, NC)), sem((2, NC)), sem((2, BACK, NC)), sem((2, BACK, NC)),
            sem((NC,)), sem((NC,)), sem((BACK, NC)), sem((BACK, NC)),
            sem((NC,)), sem((NC,)), sem((BACK, NC)), sem((BACK, NC)),
            sem((3,)), sem((3,)),
        ],
        compiler_params=pltpu.CompilerParams(
            collective_id=0, has_side_effects=True, vmem_limit_bytes=50 << 20
        ),
        name="hstu",
    )(user_lengths, cand_counts, gain_vector.reshape(1, feat), queries, key_rows, value_rows, gating, out_grad)
    return output, query_grad, key_grad, value_grad, gate_grad


def solution(mesh):
    tokens = P("ctx", "head")
    return jax.shard_map(
        per_device,
        mesh=mesh,
        in_specs=(tokens, tokens, tokens, tokens, P("head"), tokens, P(), P()),
        out_specs=(tokens,) * 5,
        check_vma=False,
    )
```

time: 219 us -> 89.7 us (0.41)
  the two profiles are of different devices: /device:TPU:186 before, /device:TPU:7 now
where the time goes in v1:
time: 89.7 us; the launch traced here: 89.4 us
  Pallas kernels  79.8 us (89%)
  local copies, waits for them, and re-layouts  8.94 us (10%)
    pallas_call x1, Pallas kernels, per_device(): pl.pallas_call(kernel, out_shape=[block] * 5, in_specs=[smem, smem, vmem,...  79.8 us
    unnamed x19, local copies, waits for them, and re-layouts  8.27 us

profile of v1, /device:TPU:7, one launch (start us, length us, event | category | flops | bytes accessed | tf_op | source)
XLA Modules:
  0.0 89.4 jit_solution(15475354620138520595)
XLA Ops:
  0.6 0.0 copy-start.6
  0.6 0.0 copy-start.5
  0.7 0.7 reshape.13.gain_ref
  1.3 0.0 copy-done.6
  1.3 0.0 copy-done.5
  1.3 0.0 copy-start
  1.3 0.9 %copy-done = bf16[512,256]{1,0:T(8,128)(2,1)S(1)} copy-done((bf16[512,256]{1,0:T(8,128)(2,1)S(1)}, bf16[512,256]{1,0:T(8,128)(2,1)}, u32[]{:S(2)}) %copy-start) | copy-done | bytes 262168
  2.3 0.0 copy-start.1
  2.3 0.9 %copy-done.1 = bf16[512,256]{1,0:T(8,128)(2,1)S(1)} copy-done((bf16[512,256]{1,0:T(8,128)(2,1)S(1)}, bf16[512,256]{1,0:T(8,128)(2,1)}, u32[]{:S(2)}) %copy-start.1) | copy-done | bytes 262168
  3.2 0.0 copy-start.2
  3.2 0.9 %copy-done.2 = bf16[512,256]{1,0:T(8,128)(2,1)S(1)} copy-done((bf16[512,256]{1,0:T(8,128)(2,1)S(1)}, bf16[512,256]{1,0:T(8,128)(2,1)}, u32[]{:S(2)}) %copy-start.2) | copy-done | bytes 262168
  4.2 0.0 copy-start.3
  4.2 0.9 %copy-done.3 = bf16[512,256]{1,0:T(8,128)(2,1)S(1)} copy-done((bf16[512,256]{1,0:T(8,128)(2,1)S(1)}, bf16[512,256]{1,0:T(8,128)(2,1)}, u32[]{:S(2)}) %copy-start.3) | copy-done | bytes 262168
  5.1 0.0 copy-start.4
  5.1 0.9 %copy-done.4 = bf16[512,256]{1,0:T(8,128)(2,1)S(1)} copy-done((bf16[512,256]{1,0:T(8,128)(2,1)S(1)}, bf16[512,256]{1,0:T(8,128)(2,1)}, u32[]{:S(2)}) %copy-start.4) | copy-done | bytes 262168
  6.1 79.8 %hstu.1 = (bf16[512,256]{1,0:T(8,128)(2,1)S(1)}, bf16[512,256]{1,0:T(8,128)(2,1)S(1)}, bf16[512,256]{1,0:T(8,128)(2,1)S(1)}, bf16[512,256]{1,0:T(8,128)(2,1)S(1)}, bf16[512,256]{1,0:T(8,128)(2,1)S(1)}) custom-call(s32[4]{0:T(128)S(1)} %copy-done.5, s32[4]{0:T(128)S(1)} %copy-done.6, bf16[1,256]{1,0:T(2,128)(2,1)S(1)} %reshape.13.gain_ref, ...), custom_call_target="tpu_custom_call" | custom-call | tf_op jit(solution)/shard_map/hstu/pallas_call | solution.py:399
  85.9 0.7 copy.18
  86.6 0.7 copy.19
  87.3 0.7 copy.20
  88.0 0.7 copy.21
  88.7 0.7 copy.22
Async XLA Ops:
  0.6 0.7 copy-start.6
  0.6 0.7 copy-start.5
  1.3 1.0 %copy-start = (bf16[512,256]{1,0:T(8,128)(2,1)S(1)}, bf16[512,256]{1,0:T(8,128)(2,1)}, u32[]{:S(2)}) copy-start(bf16[512,256]{1,0:T(8,128)(2,1)} %q_hbm.1) | copy-start | bytes 786436
  2.3 0.9 %copy-start.1 = (bf16[512,256]{1,0:T(8,128)(2,1)S(1)}, bf16[512,256]{1,0:T(8,128)(2,1)}, u32[]{:S(2)}) copy-start(bf16[512,256]{1,0:T(8,128)(2,1)} %k_hbm.1) | copy-start | bytes 786436
  3.2 0.9 %copy-start.2 = (bf16[512,256]{1,0:T(8,128)(2,1)S(1)}, bf16[512,256]{1,0:T(8,128)(2,1)}, u32[]{:S(2)}) copy-start(bf16[512,256]{1,0:T(8,128)(2,1)} %v_hbm.1) | copy-start | bytes 786436
  4.2 0.9 %copy-start.3 = (bf16[512,256]{1,0:T(8,128)(2,1)S(1)}, bf16[512,256]{1,0:T(8,128)(2,1)}, u32[]{:S(2)}) copy-start(bf16[512,256]{1,0:T(8,128)(2,1)} %gate_hbm.1) | copy-start | bytes 786436
  5.1 0.9 %copy-start.4 = (bf16[512,256]{1,0:T(8,128)(2,1)S(1)}, bf16[512,256]{1,0:T(8,128)(2,1)}, u32[]{:S(2)}) copy-start(bf16[512,256]{1,0:T(8,128)(2,1)} %og_hbm.1) | copy-start | bytes 786436

commit v2 on v0

v2 whole, which is shorter than its diff:
```python
import functools
import math

import jax
import jax.numpy as jnp
from jax import lax
from jax.experimental import pallas as pl
from jax.experimental.pallas import tpu as pltpu
from jax.sharding import PartitionSpec as P

HD = 128
D = 1024
T = 512
HALF = 256
BACK = 3
WINDOW = 1536
USERS = 4
EPS = 1e-06
SCALE = 1.0 / math.sqrt(HD)
MESH = pl.DeviceIdType.MESH
NT = (((1,), (1,)), ((), ()))
NN = (((1,), (0,)), ((), ()))
TN = (((0,), (0,)), ((), ()))
F32 = jnp.float32
BF16 = jnp.bfloat16


def dot(a, b, dims):
    return lax.dot_general(a, b, dims, preferred_element_type=F32)


def dot_exact(a, b, dims):
    return lax.dot_general(a, b, dims, preferred_element_type=F32, precision=lax.Precision.HIGHEST)


def query_bounds(pos, lengths, cands):
    seg = jnp.zeros_like(pos)
    cand = jnp.zeros_like(pos)
    start = jnp.int32(0)
    for u in range(USERS):
        length = lengths[u]
        end = start + length
        first = end - jnp.minimum(cands[u], length)
        inside = (pos >= start) & (pos < end)
        seg = jnp.where(inside, start, seg)
        cand = jnp.where(inside, first, cand)
        start = end
    return jnp.maximum(seg, pos - (WINDOW - 1)), jnp.minimum(cand, pos)


def weights(prod, allowed):
    h = prod * (0.5 * SCALE)
    w = 1.0 + jnp.tanh(h)
    a = jnp.where(allowed, w * (1.0 / WINDOW), 0.0)
    attn = (h * a).astype(BF16)
    slope = a * (0.5 + h * (1.0 - 0.5 * w))
    return attn, slope


def spans_q(d):
    if d == 0:
        return ((0, 0, HALF), (1, 0, T))
    if d == BACK:
        return ((0, 0, T), (1, HALF, HALF))
    return ((0, 0, T), (1, 0, T))


def spans_k(d):
    if d == 0:
        return ((0, 0, T), (1, HALF, HALF))
    if d == BACK:
        return ((0, 0, HALF), (1, 0, T))
    return ((0, 0, T), (1, 0, T))


def kernel(
    len_ref, cand_ref, gain_ref, q_hbm, k_hbm, v_hbm, gate_hbm, og_hbm,
    out_ref, dq_ref, dk_ref, dv_ref, dgate_ref,
    kbuf, vbuf, qbuf, dbuf, gate, og, mixed, dkacc, dvacc, back,
    slope_q, attn_k, slope_k, lo_q, hi_q, lo_k, hi_k, stats, gains,
    home_s, home_r, kv_s, kv_r, q_s, q_r, d_s, d_r, st_s, st_r, gain_s, gain_r, back_s, back_r,
):
    c = lax.axis_index("ctx")
    head = lax.axis_index("head")
    x = lax.rem(c, 4)
    core = lax.rem(head, 2)
    half = lax.rem(x, 2)
    side = x // 2
    first = c - x + 2 * core

    def device(row, place, which):
        return {"ctx": lax.rem(c - x + place + 4 * row + 128, 128), "head": head - core + which}

    partner = device(0, x, 1 - core)
    across = {"ctx": c, "head": lax.rem(head + 2, 4)}
    chips = [device(0, lax.rem(x + e, 4), core) for e in (1, 2, 3)]
    others = [device(0, lax.rem(x + e, 4), 1 - core) for e in (1, 2, 3)]
    rows = [device(r, x, k) for r in (1, -1) for k in (0, 1)]
    peers = [partner, across] + chips + others + rows
    bar = pltpu.get_barrier_semaphore()
    for p in peers:
        pl.semaphore_signal(bar, inc=1, device_id=p, device_id_type=MESH)
    pl.semaphore_wait(bar, len(peers))

    def remote(src, dst, ss, rs, dev):
        return pltpu.make_async_remote_copy(src, dst, ss, rs, device_id=dev, device_id_type=MESH)

    homes = ((k_hbm, kbuf, 3), (v_hbm, vbuf, 3), (q_hbm, qbuf, 0), (gate_hbm, gate, 0), (og_hbm, og, 0))

    def home(i, k, act):
        src, dst, base = homes[i]
        src = src.at[:, pl.ds(k * HD, HD)]
        dst = dst.at[base + half]

        @pl.when(2 * core + k != x)
        def _():
            act(remote(src, dst, home_s.at[i, k], home_r.at[i, half], device(0, 2 * core + k, side)))

    def home_local(i, k):
        src, dst, base = homes[i]

        @pl.when(2 * core + k == x)
        def _():
            pltpu.make_async_copy(src.at[:, pl.ds(k * HD, HD)], dst.at[base + half], home_r.at[i, half]).start()

    def home_wait(i, b):
        _, dst, base = homes[i]
        remote(dst.at[base + b], dst.at[base + b], home_s.at[i, 0], home_r.at[i, b], partner).wait_recv()

    for i in range(5):
        for k in range(2):
            home(i, k, lambda cp: cp.start())
            home_local(i, k)
    gains[0] = jnp.broadcast_to(gain_ref[...].astype(F32).reshape(1, 2 * HD), (8, 2 * HD))
    gain_copy = remote(gains.at[0], gains.at[1], gain_s, gain_r, partner)
    gain_copy.start()

    kv_routes = (
        (0, 0, 3, partner, 1), (0, 1, 4, partner, 2), (0, 2, 4, device(1, x, 0), 0),
        (1, 0, 3, device(1, x, 0), 1), (1, 1, 4, device(1, x, 1), 0), (1, 2, 0, partner, 2),
    )
    q_routes = (
        (0, 0, 0, device(-1, x, 1), 2), (0, 1, 1, device(-1, x, 1), 3),
        (1, 0, 0, partner, 2), (1, 1, 0, device(-1, x, 1), 4), (1, 2, 1, partner, 3), (1, 3, 2, partner, 4),
    )

    def pass_on(routes, buf, ss, rs, wanted, act):
        for which in range(2):
            todo = [r for r in routes if r[0] == which and r[2] in wanted]
            if todo:

                @pl.when(core == which)
                def _():
                    for _, number, at, to, slot in todo:
                        act(remote(buf.at[at], buf.at[slot], ss.at[number], rs.at[slot], to))

    def kv_pass(a, *wanted):
        pass_on(kv_routes, (kbuf, vbuf)[a], kv_s.at[a], kv_r.at[a], wanted, lambda cp: cp.start())

    def q_pass(*wanted):
        pass_on(q_routes, qbuf, q_s, q_r, wanted, lambda cp: cp.start())

    def d_pass(*wanted):
        pass_on(q_routes, dbuf, d_s, d_r, wanted, lambda cp: cp.start())

    def slot_wait(buf, ss, rs, slot):
        remote(buf.at[slot], buf.at[slot], ss.at[0], rs.at[slot], partner).wait_recv()

    def kv_wait(w):
        for a in range(2):
            slot_wait((kbuf, vbuf)[a], kv_s.at[a], kv_r.at[a], w)

    for b in range(2):
        pos = (first + b) * T + lax.broadcasted_iota(jnp.int32, (T, HD), 0)
        lo_q[b], hi_q[b] = query_bounds(pos, len_ref, cand_ref)
    for u in range(BACK + 2):
        pos = (first + u) * T + lax.broadcasted_iota(jnp.int32, (8, T), 1)
        lo_k[u], hi_k[u] = query_bounds(pos, len_ref, cand_ref)

    def forward(b, d):
        w = BACK + b - d
        for t, k0, kn in spans_q(d):
            r = pl.ds(t * HALF, HALF)
            prod = dot(qbuf[b, r, :], kbuf[w, pl.ds(k0, kn), :], NT)
            key = (first + b - d) * T + k0 + lax.broadcasted_iota(jnp.int32, (HALF, kn), 1)
            lo = jnp.concatenate([lo_q[b, r, :]] * (kn // HD), axis=1)
            hi = jnp.concatenate([hi_q[b, r, :]] * (kn // HD), axis=1)
            allowed = (key >= lo) & (key < hi)
            if d == 0:
                own = (first + b) * T + t * HALF + lax.broadcasted_iota(jnp.int32, (HALF, kn), 0)
                allowed = allowed | (key == own)
            attn, slope = weights(prod, allowed)
            slope_q[b, r, pl.ds(d * T + k0, kn)] = slope
            part = dot(attn, vbuf[w, pl.ds(k0, kn), :], NN)
            mixed[b, r, :] = part if d == 0 else mixed[b, r, :] + part

    def keys_before(b, d):
        u = b + d
        for t, q0, qn in spans_k(d):
            r = pl.ds(t * HALF, HALF)
            prod = dot(kbuf[BACK + b, r, :], qbuf[u, pl.ds(q0, qn), :], NT)
            key = (first + b) * T + t * HALF + lax.broadcasted_iota(jnp.int32, (HALF, qn), 0)
            allowed = (key >= lo_k[u, 0:1, pl.ds(q0, qn)]) & (key < hi_k[u, 0:1, pl.ds(q0, qn)])
            if d == 0:
                own = (first + b) * T + q0 + lax.broadcasted_iota(jnp.int32, (HALF, qn), 1)
                allowed = allowed | (key == own)
            attn, slope = weights(prod, allowed)
            attn_k[b, r, pl.ds(d * T + q0, qn)] = attn
            slope_k[b, r, pl.ds(d * T + q0, qn)] = slope

    def keys_after(b, d):
        u = b + d
        for t, q0, qn in spans_k(d):
            r = pl.ds(t * HALF, HALF)
            dm = dbuf[u, pl.ds(q0, qn), :]
            part = dot(attn_k[b, r, pl.ds(d * T + q0, qn)], dm, NN)
            dvacc[b, r, :] = part if d == 0 else dvacc[b, r, :] + part
            dattn = dot(vbuf[BACK + b, r, :], dm, NT)
            dscore = (dattn * slope_k[b, r, pl.ds(d * T + q0, qn)]).astype(BF16)
            part = dot(dscore, qbuf[u, pl.ds(q0, qn), :], NN)
            dkacc[b, r, :] = part if d == 0 else dkacc[b, r, :] + part

    def query_grad(b):
        for t in range(2):
            r = pl.ds(t * HALF, HALF)
            dm = dbuf[b, r, :]
            total = jnp.zeros((HALF, HD), F32)
            for d in range(BACK + 1):
                w = BACK + b - d
                _, k0, kn = spans_q(d)[t]
                dattn = dot(dm, vbuf[w, pl.ds(k0, kn), :], NT)
                dscore = (dattn * slope_q[b, r, pl.ds(d * T + k0, kn)]).astype(BF16)
                total += dot(dscore, kbuf[w, pl.ds(k0, kn), :], NN)
            back[1, b, r, :] = (total * SCALE).astype(BF16)

    finals = (out_ref, dq_ref, dk_ref, dv_ref, dgate_ref)

    def back_copy(i, b, act):
        dst = finals[i].at[:, pl.ds(pl.multiple_of(half * HD, HD), HD)]

        @pl.when(2 * core + b != x)
        def _():
            act(remote(back.at[i, b], dst, back_s.at[i, b], back_r.at[i, half], device(0, 2 * core + b, side)))

    def send_back(i, b):
        back_copy(i, b, lambda cp: cp.start())
        dst = finals[i].at[:, pl.ds(pl.multiple_of(half * HD, HD), HD)]

        @pl.when(2 * core + b == x)
        def _():
            pltpu.make_async_copy(back.at[i, b], dst, back_r.at[i, half]).start()

    for b in range(2):
        for a in range(2):
            home_wait(a, b)
            kv_pass(a, BACK + b)
    for b in range(2):
        home_wait(2, b)
        q_pass(b)
    forward(0, 0)
    forward(1, 0)
    forward(1, 1)

    @pl.when(core == 1)
    def _():
        kv_wait(0)

    for a in range(2):
        pass_on(kv_routes, (kbuf, vbuf)[a], kv_s.at[a], kv_r.at[a], (0,), lambda cp: cp.start())
    kv_wait(1)
    forward(0, 2)
    forward(1, 3)

    @pl.when(core == 0)
    def _():
        kv_wait(0)

    forward(0, 3)
    kv_wait(2)
    forward(0, 1)
    forward(1, 2)

    gain_copy.wait_recv()
    for i in (3, 4):
        for b in range(2):
            home_wait(i, b)
    gain = jnp.where(core == side, gains[0], gains[1])
    gain = jnp.where(half == 0, gain[0:1, :HD], gain[0:1, HD:])
    pick = lax.broadcasted_iota(jnp.int32, (8, HD), 0)
    total = jnp.zeros((8, T), F32)
    for b in range(2):
        m = mixed[b]
        dnorm = og[b].astype(F32) * gate[b].astype(F32) * gain
        for i, a in enumerate((m, m * m, dnorm, dnorm * m)):
            total += dot_exact((pick == 4 * b + i).astype(F32), a, NT)
    stats[0] = total

    def st(e):
        return remote(stats.at[0], stats.at[e], st_s.at[e - 1], st_r.at[e - 1], chips[e - 1])

    for e in range(1, 4):
        st(e).start()
    keys_before(0, 0)
    keys_before(1, 0)
    for e in range(1, 4):
        st(e).wait_recv()
    stats[4] = stats[0] + stats[1] + stats[2] + stats[3]
    st_across = remote(stats.at[4], stats.at[5], st_s.at[3], st_r.at[3], across)
    st_across.start()
    slot_wait(qbuf, q_s, q_r, 2)
    q_pass(2)
    keys_before(0, 1)
    keys_before(0, 2)
    keys_before(1, 1)
    st_across.wait_recv()
    total = stats[4] + stats[5]
    for b in range(2):
        sums = total[4 * b : 4 * b + 4]
        mean = sums[0:1] / D
        var = sums[1:2] / D - mean * mean
        rstd = lax.rsqrt(var + EPS)
        mean_one = sums[2:3] / D
        mean_two = rstd * (sums[3:4] - mean * sums[2:3]) / D
        coef = jnp.concatenate([mean, rstd, mean_one, mean_two, jnp.zeros((4, T), F32)], axis=0)
        mean, rstd, mean_one, mean_two = [dot_exact(coef, (pick == i).astype(F32), TN) for i in range(4)]
        normed = (mixed[b] - mean) * rstd
        gf = gate[b].astype(F32)
        of = og[b].astype(F32)
        dbuf[b] = (rstd * (of * gf * gain - mean_one - normed * mean_two)).astype(BF16)
        d_pass(b)
        back[0, b] = (normed * gain * gf).astype(BF16)
        back[4, b] = (of * normed * gain).astype(BF16)
        send_back(0, b)
        send_back(4, b)
    query_grad(0)
    send_back(1, 0)
    slot_wait(dbuf, d_s, d_r, 2)
    d_pass(2)
    query_grad(1)
    send_back(1, 1)
    slot_wait(qbuf, q_s, q_r, 3)
    keys_before(0, 3)
    keys_before(1, 2)
    slot_wait(qbuf, q_s, q_r, 4)
    keys_before(1, 3)
    keys_after(0, 0)
    keys_after(1, 0)
    keys_after(0, 1)
    keys_after(0, 2)
    slot_wait(dbuf, d_s, d_r, 3)
    keys_after(0, 3)

    def finish_keys(b):
        back[2, b] = (dkacc[b] * SCALE).astype(BF16)
        back[3, b] = dvacc[b].astype(BF16)
        send_back(2, b)
        send_back(3, b)

    finish_keys(0)
    keys_after(1, 1)
    keys_after(1, 2)
    slot_wait(dbuf, d_s, d_r, 4)
    keys_after(1, 3)
    finish_keys(1)

    for e in range(1, 4):
        st(e).wait_send()
    st_across.wait_send()
    gain_copy.wait_send()
    done = lambda cp: cp.wait_send()
    for a in range(2):
        pass_on(kv_routes, (kbuf, vbuf)[a], kv_s.at[a], kv_r.at[a], range(5), done)
    pass_on(q_routes, qbuf, q_s, q_r, range(5), done)
    pass_on(q_routes, dbuf, d_s, d_r, range(5), done)
    for i in range(5):
        for k in range(2):
            home(i, k, done)
            back_copy(i, k, done)
            dst = finals[i].at[:, pl.ds(k * HD, HD)]
            remote(back.at[i, k], dst, back_s.at[i, k], back_r.at[i, k], partner).wait_recv()


def write_out(*refs):
    src, dst, buf, into, out = refs[:5], refs[5:10], *refs[10:]
    reads = [pltpu.make_async_copy(src[i], buf.at[i], into.at[i]) for i in range(5)]
    writes = [pltpu.make_async_copy(buf.at[i], dst[i], out.at[i]) for i in range(5)]
    for cp in reads:
        cp.start()
    for read, write in zip(reads, writes):
        read.wait()
        write.start()
    for cp in writes:
        cp.wait()


def per_device(queries, key_rows, value_rows, gating, gain_vector, out_grad, user_lengths, cand_counts):
    feat = queries.shape[1]
    block = jax.ShapeDtypeStruct((T, feat), BF16)
    vmem = pl.BlockSpec(memory_space=pltpu.VMEM)
    smem = pl.BlockSpec(memory_space=pltpu.SMEM)
    hbm = pl.BlockSpec(memory_space=pltpu.HBM)
    sem = pltpu.SemaphoreType.DMA
    results = pl.pallas_call(
        kernel,
        out_shape=[block] * 5,
        in_specs=[smem, smem, vmem, hbm, hbm, hbm, hbm, hbm],
        out_specs=[hbm] * 5,
        scratch_shapes=[
            pltpu.VMEM((5, T, HD), BF16),
            pltpu.VMEM((5, T, HD), BF16),
            pltpu.VMEM((5, T, HD), BF16),
            pltpu.VMEM((5, T, HD), BF16),
            pltpu.VMEM((2, T, HD), BF16),
            pltpu.VMEM((2, T, HD), BF16),
            pltpu.VMEM((2, T, HD), F32),
            pltpu.VMEM((2, T, HD), F32),
            pltpu.VMEM((2, T, HD), F32),
            pltpu.VMEM((5, 2, T, HD), BF16),
            pltpu.VMEM((2, T, 4 * T), F32),
            pltpu.VMEM((2, T, 4 * T), BF16),
            pltpu.VMEM((2, T, 4 * T), F32),
            pltpu.VMEM((2, T, HD), jnp.int32),
            pltpu.VMEM((2, T, HD), jnp.int32),
            pltpu.VMEM((5, 8, T), jnp.int32),
            pltpu.VMEM((5, 8, T), jnp.int32),
            pltpu.VMEM((6, 8, T), F32),
            pltpu.VMEM((2, 8, 2 * HD), F32),
            sem((5, 2)), sem((5, 2)),
            sem((2, 3)), sem((2, 3)),
            sem((4,)), sem((5,)),
            sem((4,)), sem((5,)),
            sem((4,)), sem((4,)),
            sem, sem,
            sem((5, 2)), sem((5, 2)),
        ],
        compiler_params=pltpu.CompilerParams(
            collective_id=0, has_side_effects=True, vmem_limit_bytes=61 << 20
        ),
        name="hstu",
    )(user_lengths, cand_counts, gain_vector, queries, key_rows, value_rows, gating, out_grad)
    return pl.pallas_call(
        write_out,
        out_shape=[block] * 5,
        in_specs=[hbm] * 5,
        out_specs=[hbm] * 5,
        scratch_shapes=[pltpu.VMEM((5, T, feat), BF16), sem((5,)), sem((5,))],
        name="write_out",
    )(*results)


def solution(mesh):
    tokens = P("ctx", "head")
    return jax.shard_map(
        per_device,
        mesh=mesh,
        in_specs=(tokens, tokens, tokens, tokens, P("head"), tokens, P(), P()),
        out_specs=(tokens,) * 5,
        check_vma=False,
    )
```

time: 219 us -> 71.6 us (0.33)
  the two profiles are of different devices: /device:TPU:186 before, /device:TPU:3 now
where the time goes in v2:
time: 71.6 us; the launch traced here: 71.4 us
  Pallas kernels  70.6 us (99%)
  between operations  0.8 us (1%)
    pallas_call x1, Pallas kernels, per_device(): pl.pallas_call(kernel, out_shape=[block] * 5, in_specs=[smem, smem, vmem,...  68.5 us
    pallas_call x1, Pallas kernels, per_device(): pl.pallas_call(write_out, out_shape=[block] * 5, in_specs=[hbm] * 5, out_...  2.09 us

profile of v2, /device:TPU:3, one launch (start us, length us, event | category | flops | bytes accessed | tf_op | source)
XLA Modules:
  0.0 71.4 jit_solution(2848913131587019034)
XLA Ops:
  0.6 68.5 %hstu.1 = (bf16[512,256]{1,0:T(8,128)(2,1)}, bf16[512,256]{1,0:T(8,128)(2,1)}, bf16[512,256]{1,0:T(8,128)(2,1)}, bf16[512,256]{1,0:T(8,128)(2,1)}, bf16[512,256]{1,0:T(8,128)(2,1)}) custom-call(s32[4]{0:T(128)} %len_ref.1, s32[4]{0:T(128)} %cand_ref.1, bf16[256]{0:T(256)(128)(2,1)} %gain_ref.1, bf16[512,256]{1,0:T(8,128)(2,1)} %q_hbm.1, ...), custom_call_target="tpu_custom_call" | custom-call | tf_op jit(solution)/shard_map/hstu/pallas_call | solution.py:403
  69.2 2.1 %write_out.1 = (bf16[512,256]{1,0:T(8,128)(2,1)}, bf16[512,256]{1,0:T(8,128)(2,1)}, bf16[512,256]{1,0:T(8,128)(2,1)}, bf16[512,256]{1,0:T(8,128)(2,1)}, bf16[512,256]{1,0:T(8,128)(2,1)}) custom-call(bf16[512,256]{1,0:T(8,128)(2,1)} %get-tuple-element.10.refs_0_, bf16[512,256]{1,0:T(8,128)(2,1)} %get-tuple-element.11.refs_1_, ...), custom_call_target="tpu_custom_call" | custom-call | tf_op jit(solution)/shard_map/write_out/pallas_call | solution.py:441

commit v3 on v2

--- a/solution.py
+++ b/solution.py
@@ -76,9 +76,9 @@
 def kernel(
     len_ref, cand_ref, gain_ref, q_hbm, k_hbm, v_hbm, gate_hbm, og_hbm,
     out_ref, dq_ref, dk_ref, dv_ref, dgate_ref,
-    kbuf, vbuf, qbuf, dbuf, gate, og, mixed, dkacc, dvacc, back,
+    kbuf, vbuf, qbuf, dbuf, gate, og, mixed, dkacc, dvacc, back, placed,
     slope_q, attn_k, slope_k, lo_q, hi_q, lo_k, hi_k, stats, gains,
-    home_s, home_r, kv_s, kv_r, q_s, q_r, d_s, d_r, st_s, st_r, gain_s, gain_r, back_s, back_r,
+    home_s, home_r, kv_s, kv_r, q_s, q_r, d_s, d_r, st_s, st_r, gain_s, gain_r, back_s, back_r, own,
 ):
     c = lax.axis_index("ctx")
     head = lax.axis_index("head")
@@ -131,6 +131,9 @@
         for k in range(2):
             home(i, k, lambda cp: cp.start())
             home_local(i, k)
+    owns = [pltpu.make_async_copy(ref, placed.at[i], own.at[i]) for i, ref in ((1, gate_hbm), (2, og_hbm))]
+    for cp in owns:
+        cp.start()
     gains[0] = jnp.broadcast_to(gain_ref[...].astype(F32).reshape(1, 2 * HD), (8, 2 * HD))
     gain_copy = remote(gains.at[0], gains.at[1], gain_s, gain_r, partner)
     gain_copy.start()
@@ -233,7 +236,7 @@
                 total += dot(dscore, kbuf[w, pl.ds(k0, kn), :], NN)
             back[1, b, r, :] = (total * SCALE).astype(BF16)
 
-    finals = (out_ref, dq_ref, dk_ref, dv_ref, dgate_ref)
+    finals = (placed.at[0], dq_ref, dk_ref, dv_ref)
 
     def back_copy(i, b, act):
         dst = finals[i].at[:, pl.ds(pl.multiple_of(half * HD, HD), HD)]
@@ -250,8 +253,8 @@
         def _():
             pltpu.make_async_copy(back.at[i, b], dst, back_r.at[i, half]).start()
 
-    for b in range(2):
-        for a in range(2):
+    for a in range(2):
+        for b in range(2):
             home_wait(a, b)
             kv_pass(a, BACK + b)
     for b in range(2):
@@ -260,6 +263,9 @@
     forward(0, 0)
     forward(1, 0)
     forward(1, 1)
+    kv_wait(1)
+    forward(0, 2)
+    forward(1, 3)
 
     @pl.when(core == 1)
     def _():
@@ -267,9 +273,7 @@
 
     for a in range(2):
         pass_on(kv_routes, (kbuf, vbuf)[a], kv_s.at[a], kv_r.at[a], (0,), lambda cp: cp.start())
-    kv_wait(1)
-    forward(0, 2)
-    forward(1, 3)
+    keys_before(0, 0)
 
     @pl.when(core == 0)
     def _():
@@ -281,84 +285,109 @@
     forward(1, 2)
 
     gain_copy.wait_recv()
-    for i in (3, 4):
-        for b in range(2):
-            home_wait(i, b)
     gain = jnp.where(core == side, gains[0], gains[1])
     gain = jnp.where(half == 0, gain[0:1, :HD], gain[0:1, HD:])
     pick = lax.broadcasted_iota(jnp.int32, (8, HD), 0)
-    total = jnp.zeros((8, T), F32)
-    for b in range(2):
-        m = mixed[b]
-        dnorm = og[b].astype(F32) * gate[b].astype(F32) * gain
-        for i, a in enumerate((m, m * m, dnorm, dnorm * m)):
-            total += dot_exact((pick == 4 * b + i).astype(F32), a, NT)
-    stats[0] = total
 
     def st(e):
         return remote(stats.at[0], stats.at[e], st_s.at[e - 1], st_r.at[e - 1], chips[e - 1])
 
-    for e in range(1, 4):
-        st(e).start()
-    keys_before(0, 0)
+    st_across = remote(stats.at[4], stats.at[5], st_s.at[3], st_r.at[3], across)
+
+    def sums_along():
+        for i in (3, 4):
+            for b in range(2):
+                home_wait(i, b)
+        total = jnp.zeros((8, T), F32)
+        for b in range(2):
+            m = mixed[b]
+            dnorm = og[b].astype(F32) * gate[b].astype(F32) * gain
+            for i, a in enumerate((m, m * m, dnorm, dnorm * m)):
+                total += dot_exact((pick == 4 * b + i).astype(F32), a, NT)
+        stats[0] = total
+        for e in range(1, 4):
+            st(e).start()
+
+    def sums_across():
+        for e in range(1, 4):
+            st(e).wait_recv()
+        stats[4] = stats[0] + stats[1] + stats[2] + stats[3]
+        st_across.start()
+
+    def norm():
+        st_across.wait_recv()
+        total = stats[4] + stats[5]
+        for b in range(2):
+            sums = total[4 * b : 4 * b + 4]
+            mean = sums[0:1] / D
+            var = sums[1:2] / D - mean * mean
+            rstd = lax.rsqrt(var + EPS)
+            mean_one = sums[2:3] / D
+            mean_two = rstd * (sums[3:4] - mean * sums[2:3]) / D
+            coef = jnp.concatenate([mean, rstd, mean_one, mean_two, jnp.zeros((4, T), F32)], axis=0)
+            mean, rstd, mean_one, mean_two = [dot_exact(coef, (pick == i).astype(F32), TN) for i in range(4)]
+            normed = (mixed[b] - mean) * rstd
+            dnorm = og[b].astype(F32) * gate[b].astype(F32) * gain
+            dbuf[b] = (rstd * (dnorm - mean_one - normed * mean_two)).astype(BF16)
+            d_pass(b)
+            back[0, b] = normed.astype(BF16)
+        for b in range(2):
+            send_back(0, b)
+
+    def back_wait(i):
+        for k in range(2):
+            dst = finals[i].at[:, pl.ds(k * HD, HD)]
+            remote(back.at[i, k], dst, back_s.at[i, k], back_r.at[i, k], partner).wait_recv()
+
+    writes = [pltpu.make_async_copy(placed.at[i], ref, own.at[i]) for i, ref in ((3, out_ref), (4, dgate_ref))]
+
+    def gated():
+        back_wait(0)
+        for cp in owns:
+            cp.wait()
+        normed = placed[0].astype(F32)
+        gain = gains[0, 0:1, :]
+        placed[3] = (normed * gain * placed[1].astype(F32)).astype(BF16)
+        placed[4] = (placed[2].astype(F32) * normed * gain).astype(BF16)
+        for cp in writes:
+            cp.start()
+
+    def finish_keys(b):
+        back[2, b] = (dkacc[b] * SCALE).astype(BF16)
+        back[3, b] = dvacc[b].astype(BF16)
+        send_back(2, b)
+        send_back(3, b)
+
+    sums_along()
     keys_before(1, 0)
-    for e in range(1, 4):
-        st(e).wait_recv()
-    stats[4] = stats[0] + stats[1] + stats[2] + stats[3]
-    st_across = remote(stats.at[4], stats.at[5], st_s.at[3], st_r.at[3], across)
-    st_across.start()
+    keys_before(0, 1)
+    sums_across()
     slot_wait(qbuf, q_s, q_r, 2)
     q_pass(2)
-    keys_before(0, 1)
     keys_before(0, 2)
     keys_before(1, 1)
-    st_across.wait_recv()
-    total = stats[4] + stats[5]
-    for b in range(2):
-        sums = total[4 * b : 4 * b + 4]
-        mean = sums[0:1] / D
-        var = sums[1:2] / D - mean * mean
-        rstd = lax.rsqrt(var + EPS)
-        mean_one = sums[2:3] / D
-        mean_two = rstd * (sums[3:4] - mean * sums[2:3]) / D
-        coef = jnp.concatenate([mean, rstd, mean_one, mean_two, jnp.zeros((4, T), F32)], axis=0)
-        mean, rstd, mean_one, mean_two = [dot_exact(coef, (pick == i).astype(F32), TN) for i in range(4)]
-        normed = (mixed[b] - mean) * rstd
-        gf = gate[b].astype(F32)
-        of = og[b].astype(F32)
-        dbuf[b] = (rstd * (of * gf * gain - mean_one - normed * mean_two)).astype(BF16)
-        d_pass(b)
-        back[0, b] = (normed * gain * gf).astype(BF16)
-        back[4, b] = (of * normed * gain).astype(BF16)
-        send_back(0, b)
-        send_back(4, b)
-    query_grad(0)
-    send_back(1, 0)
-    slot_wait(dbuf, d_s, d_r, 2)
-    d_pass(2)
-    query_grad(1)
-    send_back(1, 1)
     slot_wait(qbuf, q_s, q_r, 3)
     keys_before(0, 3)
     keys_before(1, 2)
     slot_wait(qbuf, q_s, q_r, 4)
     keys_before(1, 3)
+    norm()
     keys_after(0, 0)
     keys_after(1, 0)
     keys_after(0, 1)
+    query_grad(0)
+    send_back(1, 0)
+    slot_wait(dbuf, d_s, d_r, 2)
+    d_pass(2)
     keys_after(0, 2)
+    keys_after(1, 1)
     slot_wait(dbuf, d_s, d_r, 3)
     keys_after(0, 3)
-
-    def finish_keys(b):
-        back[2, b] = (dkacc[b] * SCALE).astype(BF16)
-        back[3, b] = dvacc[b].astype(BF16)
-        send_back(2, b)
-        send_back(3, b)
-
     finish_keys(0)
-    keys_after(1, 1)
+    query_grad(1)
+    send_back(1, 1)
     keys_after(1, 2)
+    gated()
     slot_wait(dbuf, d_s, d_r, 4)
     keys_after(1, 3)
     finish_keys(1)
@@ -375,9 +404,12 @@
     for i in range(5):
         for k in range(2):
             home(i, k, done)
-            back_copy(i, k, done)
-            dst = finals[i].at[:, pl.ds(k * HD, HD)]
-            remote(back.at[i, k], dst, back_s.at[i, k], back_r.at[i, k], partner).wait_recv()
+            if i < 4:
+                back_copy(i, k, done)
+    for i in (1, 2, 3):
+        back_wait(i)
+    for cp in writes:
+        cp.wait()
 
 
 def write_out(*refs):
@@ -415,7 +447,8 @@
             pltpu.VMEM((2, T, HD), F32),
             pltpu.VMEM((2, T, HD), F32),
             pltpu.VMEM((2, T, HD), F32),
-            pltpu.VMEM((5, 2, T, HD), BF16),
+            pltpu.VMEM((4, 2, T, HD), BF16),
+            pltpu.VMEM((5, T, feat), BF16),
             pltpu.VMEM((2, T, 4 * T), F32),
             pltpu.VMEM((2, T, 4 * T), BF16),
             pltpu.VMEM((2, T, 4 * T), F32),
@@ -431,7 +464,8 @@
             sem((4,)), sem((5,)),
             sem((4,)), sem((4,)),
             sem, sem,
-            sem((5, 2)), sem((5, 2)),
+            sem((4, 2)), sem((4, 2)),
+            sem((5,)),
         ],
         compiler_params=pltpu.CompilerParams(
             collective_id=0, has_side_effects=True, vmem_limit_bytes=61 << 20

time: 71.6 us -> 70.5 us (0.985)
  Pallas kernels: 70.6 us -> 69.6 us
    pallas_call x1, Pallas kernels: 68.5 us -> 67.5 us  [per_device(): pl.pallas_call(kernel, out_shape=[block] * 5, in_specs=[smem, smem, vmem,...]
where the time goes in v3:
time: 70.5 us; the launch traced here: 70.4 us
  Pallas kernels  69.6 us (99%)
  between operations  0.8 us (1%)
    pallas_call x1, Pallas kernels, per_device(): pl.pallas_call(kernel, out_shape=[block] * 5, in_specs=[smem, smem, vmem,...  67.5 us
    pallas_call x1, Pallas kernels, per_device(): pl.pallas_call(write_out, out_shape=[block] * 5, in_specs=[hbm] * 5, out_...  2.09 us

profile of v3, /device:TPU:3, one launch (start us, length us, event | category | flops | bytes accessed | tf_op | source)
XLA Modules:
  0.0 70.4 jit_solution(18322559773127971412)
XLA Ops:
  0.6 67.5 %hstu.1 = (bf16[512,256]{1,0:T(8,128)(2,1)}, bf16[512,256]{1,0:T(8,128)(2,1)}, bf16[512,256]{1,0:T(8,128)(2,1)}, bf16[512,256]{1,0:T(8,128)(2,1)}, bf16[512,256]{1,0:T(8,128)(2,1)}) custom-call(s32[4]{0:T(128)} %len_ref.1, s32[4]{0:T(128)} %cand_ref.1, bf16[256]{0:T(256)(128)(2,1)} %gain_ref.1, bf16[512,256]{1,0:T(8,128)(2,1)} %q_hbm.1, ...), custom_call_target="tpu_custom_call" | custom-call | tf_op jit(solution)/shard_map/hstu/pallas_call | solution.py:435
  68.1 2.1 %write_out.1 = (bf16[512,256]{1,0:T(8,128)(2,1)}, bf16[512,256]{1,0:T(8,128)(2,1)}, bf16[512,256]{1,0:T(8,128)(2,1)}, bf16[512,256]{1,0:T(8,128)(2,1)}, bf16[512,256]{1,0:T(8,128)(2,1)}) custom-call(bf16[512,256]{1,0:T(8,128)(2,1)} %get-tuple-element.10.refs_0_, bf16[512,256]{1,0:T(8,128)(2,1)} %get-tuple-element.11.refs_1_, ...), custom_call_target="tpu_custom_call" | custom-call | tf_op jit(solution)/shard_map/write_out/pallas_call | solution.py:475

commit v4 on v3

--- a/solution.py
+++ b/solution.py
@@ -96,7 +96,7 @@
     chips = [device(0, lax.rem(x + e, 4), core) for e in (1, 2, 3)]
     others = [device(0, lax.rem(x + e, 4), 1 - core) for e in (1, 2, 3)]
     rows = [device(r, x, k) for r in (1, -1) for k in (0, 1)]
-    peers = [partner, across] + chips + others + rows
+    peers = [across] + rows + chips + others + [partner]
     bar = pltpu.get_barrier_semaphore()
     for p in peers:
         pl.semaphore_signal(bar, inc=1, device_id=p, device_id_type=MESH)
@@ -269,10 +269,11 @@
 
     @pl.when(core == 1)
     def _():
-        kv_wait(0)
-
-    for a in range(2):
-        pass_on(kv_routes, (kbuf, vbuf)[a], kv_s.at[a], kv_r.at[a], (0,), lambda cp: cp.start())
+        for a in range(2):
+            buf = (kbuf, vbuf)[a]
+            slot_wait(buf, kv_s.at[a], kv_r.at[a], 0)
+            remote(buf.at[0], buf.at[2], kv_s.at[a, 2], kv_r.at[a, 2], partner).start()
+
     keys_before(0, 0)
 
     @pl.when(core == 0)
@@ -353,10 +354,10 @@
             cp.start()
 
     def finish_keys(b):
+        back[3, b] = dvacc[b].astype(BF16)
+        send_back(3, b)
         back[2, b] = (dkacc[b] * SCALE).astype(BF16)
-        back[3, b] = dvacc[b].astype(BF16)
         send_back(2, b)
-        send_back(3, b)
 
     sums_along()
     keys_before(1, 0)

time: 70.5 us -> 70.6 us (level)
  no operation moved by 1% of the time
where the time goes in v4:
time: 70.6 us; the launch traced here: 70.4 us
  Pallas kernels  69.6 us (99%)
  between operations  0.8 us (1%)
    pallas_call x1, Pallas kernels, per_device(): pl.pallas_call(kernel, out_shape=[block] * 5, in_specs=[smem, smem, vmem,...  67.5 us
    pallas_call x1, Pallas kernels, per_device(): pl.pallas_call(write_out, out_shape=[block] * 5, in_specs=[hbm] * 5, out_...  2.09 us

profile of v4, /device:TPU:3, one launch (start us, length us, event | category | flops | bytes accessed | tf_op | source)
XLA Modules:
  0.0 70.4 jit_solution(12606180843027219618)
XLA Ops:
  0.6 67.5 %hstu.1 = (bf16[512,256]{1,0:T(8,128)(2,1)}, bf16[512,256]{1,0:T(8,128)(2,1)}, bf16[512,256]{1,0:T(8,128)(2,1)}, bf16[512,256]{1,0:T(8,128)(2,1)}, bf16[512,256]{1,0:T(8,128)(2,1)}) custom-call(s32[4]{0:T(128)} %len_ref.1, s32[4]{0:T(128)} %cand_ref.1, bf16[256]{0:T(256)(128)(2,1)} %gain_ref.1, bf16[512,256]{1,0:T(8,128)(2,1)} %q_hbm.1, ...), custom_call_target="tpu_custom_call" | custom-call | tf_op jit(solution)/shard_map/hstu/pallas_call | solution.py:436
  68.1 2.1 %write_out.1 = (bf16[512,256]{1,0:T(8,128)(2,1)}, bf16[512,256]{1,0:T(8,128)(2,1)}, bf16[512,256]{1,0:T(8,128)(2,1)}, bf16[512,256]{1,0:T(8,128)(2,1)}, bf16[512,256]{1,0:T(8,128)(2,1)}) custom-call(bf16[512,256]{1,0:T(8,128)(2,1)} %get-tuple-element.10.refs_0_, bf16[512,256]{1,0:T(8,128)(2,1)} %get-tuple-element.11.refs_1_, ...), custom_call_target="tpu_custom_call" | custom-call | tf_op jit(solution)/shard_map/write_out/pallas_call | solution.py:476
